TPU v7x, 256 devices: a whole 4x4x8 slice. The times are simulated.
256 devices in a mesh: seq: 64 (over z, y, core), head: 4 (over x).
Axes of the slice: x: 4, y: 4, z: 8, core: 2. Of those that a mesh axis runs over, the one named last changes fastest.
Arguments:
- queries: bfloat16 [32768, 2048], P('seq', 'head'), may hold values from -8.4 to 8.4, as said below
- keyval: bfloat16 [2, 32768, 512], P(None, 'seq', 'head'), may hold values from -16 to 16, as said below
- gates: int32 [64, 8], replicated, may hold values from -1 to 63, as said below
- pair_block: int32 [32], replicated, may hold values from 0 to 31, each once
- out_weight: bfloat16 [2048, 4096], P('head'), may hold values from -0.125 to 0.125
Outputs:
- layer_out: bfloat16 [32768, 4096], P(('seq', 'head'))
Inputs may be any that keep to these rules, and one draw needn't show every extreme that they name: Values of queries lie within the bounds. Values of keyval lie within the bounds. `gates`: row b names distinct blocks at or before b; its first entry is b itself; unused entries are -1 and follow the used ones. For every b < 32 and every k < 32 with k != b, the rows b and 63 - b together name at most one of the blocks k and 63 - k.
All inputs are finite; a program needn't handle non-finite values.
Results may differ from a plain program's by a relative error of at most 0.0053.
Values may be sent and summed in bfloat16 or wider, within the bound.
A program may use at most 128 MiB of HBM per device.

v0:
```python
import jax
import jax.numpy as jnp
from jax import lax
from jax.sharding import PartitionSpec as P

HEADS = 16
KVH = 4
HD = 128
TOPK = 8


def attend(query_rows, picked, entries, own_block, offset):
    key_span = picked.shape[1]
    half_rows = query_rows.shape[0]
    per_entry = key_span // entries.shape[0]
    scores = jnp.einsum(
        "qkgd,lkd->kgql", query_rows, picked[0], preferred_element_type=jnp.float32
    ) / jnp.sqrt(jnp.float32(HD))
    listed = jnp.broadcast_to(entries[:, None], (entries.shape[0], per_entry)).reshape(key_span)
    key_pos = jnp.arange(key_span, dtype=jnp.int32) % per_entry
    query_pos = offset + jnp.arange(half_rows, dtype=jnp.int32)
    allowed = (listed >= 0)[None, :] & (
        (listed != own_block)[None, :] | (key_pos[None, :] <= query_pos[:, None])
    )
    masked = jnp.where(allowed, scores, jnp.float32(-1e30))
    row_peak = jnp.max(masked, axis=-1, keepdims=True)
    weights = jnp.where(allowed, jnp.exp(masked - row_peak), jnp.float32(0.0))
    row_total = jnp.sum(weights, axis=-1)
    rounded = weights.astype(jnp.bfloat16)
    blended = jnp.einsum("kgql,lkd->qkgd", rounded, picked[1], preferred_element_type=jnp.float32)
    blended = blended / jnp.transpose(row_total, (2, 0, 1))[..., None]
    return blended.reshape(half_rows, -1).astype(jnp.bfloat16)


def rows_of(block_ids, gates, blocks):
    block_range = jnp.arange(blocks, dtype=jnp.int32)
    one_hot = block_range[None, :] == block_ids[:, None]
    return jnp.sum(jnp.where(one_hot[:, :, None], gates[None, :, :], 0), axis=1)


def body(queries, keyval, gates, pair_block, out_weight):
    seq_count = lax.axis_size("seq")
    seq_index = lax.axis_index("seq")
    half_rows = queries.shape[0] // 2
    row_width = keyval.shape[2]
    kv_local = row_width // HD
    group_size = HEADS // KVH
    my_pair = seq_index // 2
    my_half = seq_index % 2
    pair_range = jnp.arange(seq_count // 2, dtype=jnp.int32)
    early_block = jnp.sum(jnp.where(pair_range == my_pair, pair_block, 0))
    own_blocks = jnp.stack([early_block, seq_count - 1 - early_block])
    own_lists = rows_of(own_blocks, gates, seq_count)
    match_early = own_lists[:, :, None] == pair_block[None, None, :]
    match_late = own_lists[:, :, None] == (seq_count - 1 - pair_block)[None, None, :]
    owner_pair = jnp.sum(jnp.where(match_early | match_late, pair_range, 0), axis=-1)
    slot_side = jnp.sum(jnp.where(match_late, 1, 0), axis=-1)
    halves = jnp.arange(2, dtype=jnp.int32)
    gathered = lax.all_gather(keyval, "seq", axis=1, tiled=True)
    kv_table = gathered.reshape(2, 2 * seq_count, half_rows, row_width)
    piece_index = (2 * owner_pair[:, :, None] + halves) * 2 + slot_side[:, :, None]
    picked = jnp.take(kv_table, piece_index.reshape(-1), axis=1)
    picked = picked.reshape(2, 2, TOPK * 2 * half_rows, kv_local, HD)
    query_blocks = queries.reshape(2, half_rows, kv_local, group_size, HD)
    results = []
    for side_index in range(2):
        results.append(
            attend(
                query_blocks[side_index],
                picked[:, side_index],
                own_lists[side_index],
                own_blocks[side_index],
                my_half * half_rows,
            )
        )
    attended = jnp.concatenate(results, axis=0)
    summed = lax.psum_scatter(
        jnp.dot(attended, out_weight, preferred_element_type=jnp.float32),
        "head",
        scatter_dimension=0,
        tiled=True,
    )
    return summed.astype(jnp.bfloat16)


def solution(mesh):
    placed = (P("seq", "head"), P(None, "seq", "head"), P(), P(), P("head", None))
    return jax.shard_map(
        body, mesh=mesh, in_specs=placed, out_specs=P(("seq", "head"), None), check_vma=False
    )
```

profile of v0, /device:TPU:1, one launch (start us, length us, event | category | flops | bytes accessed | tf_op | source)
XLA Modules:
  0.0 252.3 jit_solution(14247261059974003888)
XLA Ops:
  6.5 0.0 all-gather.2.cloned.1.call-start
  6.5 0.7 all-gather.2.cloned.1.call-update
  7.3 0.0 reduce-scatter.2.cloned.1.call-start
  7.3 1.3 fusion.44
  9.3 0.7 pad_add_fusion
  10.0 0.1 iota_compare_fusion
  10.1 0.8 select_reduce_fusion.1
  10.9 0.9 select_reduce_fusion
  11.8 0.1 multiply_add_fusion
  11.9 0.1 add.112
  11.9 0.1 add.109
  12.0 0.7 compare_bitcast_fusion.3
  12.7 0.1 broadcast_bitcast_fusion.3
  12.8 0.1 broadcast_bitcast_fusion
  12.9 0.1 broadcast_bitcast_fusion.1
  13.0 1.1 fusion.53
  14.1 0.1 copy.38
  14.2 0.1 copy.39
  14.4 4.3 %fusion.14 = (pred[256,4096]{0,1:T(8,128)(4,1)S(1)}, pred[256,4096]{0,1:T(8,128)(4,1)S(1)}) fusion(s32[256]{0:T(256)S(1)} %iota_add_fusion, s32[4096]{0:T(1024)S(1)} %add_select_fusion, pred[4096]{0:T(1024)(128)(4,1)S(1)} %bitcast.163, pred[4096]{0:T(1024)(128)(4,1)S(1)} %bitcast.164, pred[4096]{0:T(1024)(128)(4,1)S(1)} %bitcast.165, ...), kind=kLoop, calls=%fused_computation.19 | loop fusion | flops 5242880 | bytes 2130944 | tf_op jit(solution)/shard_map/and | solution.py:22
  18.7 95.6 %all-gather.2.cloned.1.call-done = bf16[2,32768,128]{2,1,0:T(8,128)(2,1)} async-done(((bf16[2,512,128]{2,1,0:T(8,128)(2,1)}), bf16[2,32768,128]{2,1,0:T(8,128)(2,1)}) %all-gather.2.cloned.1.call-update) | async-done | bytes 16777232 | tf_op jit(solution)/shard_map/all_gather | solution.py:59
  114.3 8.8 %gather_fusion = bf16[32,2,256,128]{3,2,1,0:T(8,128)(2,1)} fusion(bf16[2,128,256,128]{3,2,1,0:T(8,128)(2,1)} %bitcast.157, s32[1024]{0:T(1024)S(1)} %pad_clamp_fusion), kind=kCustom, calls=%fused_computation | custom fusion | bytes 8388736 | tf_op jit(solution)/shard_map/jit(_take)/gather | solution.py:62
  123.1 2.5 copy.21
  125.6 3.2 %broadcast_select_fusion = bf16[2,2,4096,1,128]{4,2,3,1,0:T(8,128)(2,1)S(1)} fusion(bf16[2,2,4096,1,128]{4,2,3,1,0:T(8,128)(2,1)S(1)} %bitcast.156, pred[2,4096]{1,0:T(4,128)(4,1)S(1)} %bitcast.162), kind=kLoop, calls=%fused_computation.21 | loop fusion | flops 2097152 | bytes 8396800 | tf_op jit(solution)/shard_map/jit(_take)/select_n | solution.py:62
  128.8 0.0 copy-start.1
  128.8 1.9 copy-done.1
  130.7 2.7 %fusion = (f32[4,256]{1,0:T(4,128)S(1)}, f32[4096,256,4]{1,0,2:T(8,128)S(1)}) fusion(pred[256,4096]{0,1:T(8,128)(4,1)S(1)} %get-tuple-element.9, bf16[256,4,128]{0,2,1:T(8,128)(2,1)S(1)} %bitcast.161, bf16[2,2,4096,1,128]{4,2,3,1,0:T(8,128)(2,1)S(1)} %broadcast_select_fusion), kind=kOutput, calls=%fused_computation.5 | convolution fusion | flops 1086323712 | bytes 19140608 | tf_op jit(solution)/shard_map/qkgd,lkd->kgql/dot_general | solution.py:16
  133.4 4.2 %fusion.2 = f32[4,256]{1,0:T(4,128)S(1)} fusion(f32[4096,256,4]{1,0,2:T(8,128)S(1)} %get-tuple-element.20, f32[4,256]{1,0:T(4,128)S(1)} %get-tuple-element.19, pred[256,4096]{0,1:T(8,128)(4,1)S(1)} %get-tuple-element.9), kind=kLoop, calls=%fused_computation.7 | loop fusion | flops 20970496 | bytes 17833984 | tf_op jit(solution)/shard_map/reduce_sum | solution.py:28
  137.6 5.6 %fusion.27 = bf16[256,1,4,128]{0,3,2,1:T(8,128)(2,1)S(1)} fusion(f32[4096,256,4]{1,0,2:T(8,128)S(1)} %get-tuple-element.20, f32[4,256]{1,0:T(4,128)S(1)} %get-tuple-element.19, pred[256,4096]{0,1:T(8,128)(4,1)S(1)} %get-tuple-element.9, bf16[2,2,4096,1,128]{4,2,3,1,0:T(8,128)(2,1)} %copy-done.1, f32[256,4]{0,1:T(4,128)S(1)} %bitcast.168), kind=kOutput, calls=%fused_computation.31 | convolution fusion | flops 1094975488 | bytes 19144704 | tf_op jit(solution)/shard_map/kgql,lkd->qkgd/dot_general | solution.py:30
  143.2 3.9 %fusion.1 = (f32[4,256]{1,0:T(4,128)S(1)}, f32[4096,256,4]{1,0,2:T(8,128)S(1)}) fusion(pred[256,4096]{0,1:T(8,128)(4,1)S(1)} %get-tuple-element.10, bf16[256,4,128]{0,2,1:T(8,128)(2,1)S(1)} %bitcast.160, bf16[2,2,4096,1,128]{4,2,3,1,0:T(8,128)(2,1)} %copy-done.1), kind=kOutput, calls=%fused_computation.6 | convolution fusion | flops 1086323712 | bytes 19140608 | tf_op jit(solution)/shard_map/qkgd,lkd->kgql/dot_general | solution.py:16
  147.2 4.4 %fusion.4 = f32[4,256]{1,0:T(4,128)S(1)} fusion(f32[4096,256,4]{1,0,2:T(8,128)S(1)} %get-tuple-element.18, f32[4,256]{1,0:T(4,128)S(1)} %get-tuple-element.17, pred[256,4096]{0,1:T(8,128)(4,1)S(1)} %get-tuple-element.10), kind=kLoop, calls=%fused_computation.9 | loop fusion | flops 20970496 | bytes 17833984 | tf_op jit(solution)/shard_map/reduce_sum | solution.py:28
  151.5 0.0 copy-start
  151.5 5.7 %fusion.33 = bf16[256,1,4,128]{0,3,2,1:T(8,128)(2,1)S(1)} fusion(f32[4096,256,4]{1,0,2:T(8,128)S(1)} %get-tuple-element.18, f32[4,256]{1,0:T(4,128)S(1)} %get-tuple-element.17, pred[256,4096]{0,1:T(8,128)(4,1)S(1)} %get-tuple-element.10, bf16[2,2,4096,1,128]{4,2,3,1,0:T(8,128)(2,1)} %copy-done.1, f32[256,4]{0,1:T(4,128)S(1)} %bitcast.167), kind=kOutput, calls=%fused_computation.33 | convolution fusion | flops 1094975488 | bytes 19144704 | tf_op jit(solution)/shard_map/kgql,lkd->qkgd/dot_general | solution.py:30
  157.3 0.0 copy-done
  157.3 5.7 %fusion.36 = f32[512,4096]{1,0:T(8,128)} fusion(bf16[512,4096]{1,0:T(8,128)(2,1)S(1)} %copy-done, bf16[256,512]{0,1:T(8,128)(2,1)S(1)} %bitcast.159, bf16[256,512]{0,1:T(8,128)(2,1)S(1)} %bitcast.158), kind=kOutput, calls=%fused_computation.34 | convolution fusion | flops 2148532224 | bytes 13107200 | tf_op jit(solution)/shard_map/dot_general | solution.py:78
  162.9 0.0 reduce-scatter.2.cloned.1.call-update
  163.0 79.8 %reduce-scatter.2.cloned.1.call-done = f32[128,4096]{1,0:T(8,128)} async-done(((f32[512,4096]{1,0:T(8,128)}), f32[128,4096]{1,0:T(8,128)}) %reduce-scatter.2.cloned.1.call-update) | async-done | bytes 2097168 | tf_op jit(solution)/shard_map/reduce_scatter | solution.py:77
  242.8 2.7 %convert_element_type.27 = bf16[128,4096]{1,0:T(8,128)(2,1)} convert(f32[128,4096]{1,0:T(8,128)} %reduce-scatter.2.cloned.1.call-done) | non-fusion elementwise | flops 524288 | bytes 3145728 | tf_op jit(solution)/shard_map/convert_element_type | solution.py:83
  (11 shorter events, 0.1 us)
Async XLA Ops:
  6.5 107.8 %all-gather.2.cloned.1.call-start = ((), (), s32[]{:S(2)}) async-start(), calls=%async_computation.1 | async-start | bytes 17039360 | tf_op jit(solution)/shard_map/all_gather | solution.py:59
  7.3 235.5 %reduce-scatter.2.cloned.1.call-start = ((), (), s32[]{:S(2)}) async-start(), calls=%async_computation.2 | async-start | bytes 10485760 | tf_op jit(solution)/shard_map/reduce_scatter | solution.py:77
  128.8 1.9 copy-start.1
  151.5 5.7 %copy-start = (bf16[512,4096]{1,0:T(8,128)(2,1)S(1)}, bf16[512,4096]{1,0:T(8,128)(2,1)}, u32[]{:S(2)}) copy-start(bf16[512,4096]{1,0:T(8,128)(2,1)} %param.9) | copy-start | bytes 12582916
Sparse Core Ops, SparseCore 0:
  10.2 104.1 all-gather.1
  163.1 79.6 reduce-scatter.1
where the time goes:
time: 253 us; the launch traced here: 252 us
  waiting for transfers between devices  176 us (70%)
  matrix products  23.6 us (9%)
  other arithmetic  23.3 us (9%)
  local copies, waits for them, and re-layouts  14.9 us (6%)
  between operations  14.3 us (6%)
    all_gather x1, waiting for transfers between devices, body(): gathered = lax.all_gather(keyval, 'seq', axis=1, tiled=True)  95.6 us
    reduce_scatter x1, waiting for transfers between devices, body(): lax.psum_scatter(jnp.dot(attended, out_weight, preferred_element_type=jnp...  79.8 us
    dot_general x2, matrix products, attend(): jnp.einsum('kgql,lkd->qkgd', rounded, picked[1], preferred_element_type=j...  11.3 us
    gather x2, local copies, waits for them, and re-layouts, body(): picked = jnp.take(kv_table, piece_index.reshape(-1), axis=1)  11.2 us
    reduce_sum x2, other arithmetic, attend(): row_total = jnp.sum(weights, axis=-1)  8.54 us
    dot_general x2, matrix products, attend(): jnp.einsum('qkgd,lkd->kgql', query_rows, picked[0], preferred_element_typ...  6.65 us
    dot_general x1, matrix products, body(): jnp.dot(attended, out_weight, preferred_element_type=jnp.float32)  5.66 us
  transfers between devices with their start and end apart: 2, of which 2 were waited for; matrix products, arithmetic and copies ran while one was open for 4% of the time, Pallas kernels for 0%

commit v1 on v0

v1 whole, which is shorter than its diff:
```python
import jax
import jax.numpy as jnp
from jax import lax
from jax.experimental import pallas as pl
from jax.experimental.pallas import tpu as pltpu
from jax.sharding import PartitionSpec as P

HD = 128
TOPK = 8
HALF = 256
R1 = 192
R2 = HALF - R1
NZ, NY, NX = 8, 4, 4
SCALE = 1.4426950408889634 / 128**0.5
NEG = -1e30
BIG = 1e30
WCH = ((0, 512), (512, 512), (1024, 512), (1536, 512))
ORDER = (2, 1, 3, 0)
f32, bf16 = jnp.float32, jnp.bfloat16


def mod(a, n):
    return lax.rem(a, jnp.int32(n))


def dot_nt(a, b):
    return lax.dot_general(a, b, (((1,), (1,)), ((), ())), preferred_element_type=f32)


def kernel(gates, pb, q, kvin, w, o, sel_k, sel_v, col_k, col_v, row_k, row_v, st1_k, st1_v, st2_k, st2_v,
           wbuf, s_acc, p_buf, l_buf, att_s, attg, bits, slots, valid,
           z1s, z1r, y2s, y2r, y1s, y1r, z2s, z2r, sbs, sbr, wss, wsr, wfs, wfr, wbs, wbr, ats, atr, wls):
    s = lax.axis_index("seq").astype(jnp.int32)
    x = lax.axis_index("head").astype(jnp.int32)
    z = lax.div(s, jnp.int32(8))
    y = mod(lax.div(s, jnp.int32(2)), 4)
    c = mod(s, 2)
    me = z * 4 + y
    sel, col, row = (sel_k, sel_v), (col_k, col_v), (row_k, row_v)
    st1, st2 = (st1_k, st1_v), (st2_k, st2_v)
    base = pl.multiple_of(c * HALF, HALF)

    def dev(zz, yy, cc, xx):
        return ((zz * 4 + yy) * 2 + cc, xx)

    def remote(src, dst, ssem, rsem, device):
        return pltpu.make_async_remote_copy(
            src_ref=src, dst_ref=dst, send_sem=ssem, recv_sem=rsem,
            device_id=device, device_id_type=pl.DeviceIdType.MESH)

    def z1(k, way, hop):
        step = 1 if way == 0 else NZ - 1
        zo = mod(z + (NZ - step) * (hop - 1), NZ)
        lo, n = (0, R1) if hop < 4 else ((0, R1 // 2) if way == 0 else (R1 // 2, R1 // 2))
        src = kvin.at[k, :, 0:R1] if hop == 1 else col[k].at[zo, :, lo:lo + n]
        return remote(src, col[k].at[zo, :, lo:lo + n], z1s.at[k, way, hop - 1], z1r.at[k, way, hop - 1],
                      dev(mod(z + step, NZ), y, c, x))

    def y2(k, d):
        return remote(kvin.at[k, :, R1:HALF], row[k].at[y], y2s.at[k, d - 1], y2r.at[k, d - 1],
                      dev(z, mod(y + d, NY), c, x))

    def y1(k, r, d):
        slot = mod(z + r, NZ) * 4 + y
        return remote(st1[k].at[r, d - 1], sel[k].at[slot, pl.ds(base, R1)], y1s.at[k, r, d - 1],
                      y1r.at[k, r, d - 1], dev(z, mod(y + d, NY), c, x))

    def z2(k, r, j):
        slot = z * 4 + mod(y + j, NY)
        return remote(st2[k].at[r, j], sel[k].at[slot, pl.ds(base + R1, R2)], z2s.at[k, r, j],
                      z2r.at[k, r, j], dev(mod(z + r, NZ), y, c, x))

    def sib(k, r):
        at = sel[k].at[pl.ds(mod(z + r, NZ) * 4, 4), pl.ds(base, HALF)]
        return remote(at, at, sbs.at[k, r], sbr.at[k, r], dev(z, y, 1 - c, x))

    def sib_own(k):
        at = sel[k].at[32, pl.ds(base, HALF)]
        return remote(at, at, sbs.at[k, 8], sbr.at[k, 8], dev(z, y, 1 - c, x))

    def wcols(i):
        off, n = WCH[i]
        return pl.ds(pl.multiple_of(c * 2048 + off, 128), n)

    def w1(way, i):
        step = 1 if way == 0 else NX - 1
        return remote(w.at[:, wcols(i)], wbuf.at[x, :, wcols(i)], wss.at[way, i], wsr.at[way, i],
                      dev(z, y, c, mod(x + step, NX)))

    def w2(way, i):
        step = 1 if way == 0 else NX - 1
        at = wbuf.at[mod(x + NX - step, NX), way * 256:way * 256 + 256, wcols(i)]
        return remote(at, at, wfs.at[way, i], wfr.at[way, i], dev(z, y, c, mod(x + step, NX)))

    def wsib(d, i):
        at = wbuf.at[mod(x + d, NX), :, wcols(i)]
        return remote(at, at, wbs.at[d - 1, i], wbr.at[d - 1, i], dev(z, y, 1 - c, x))

    def send_att(d):
        return remote(att_s.at[d - 1], attg.at[x], ats.at[d - 1], atr.at[d - 1], dev(z, y, c, mod(x + d, NX)))

    bar = pltpu.get_barrier_semaphore()
    peers = [dev(mod(z + r, NZ), y, c, x) for r in range(1, NZ)]
    peers += [dev(z, mod(y + d, NY), c, x) for d in range(1, NY)]
    peers += [dev(z, y, c, mod(x + d, NX)) for d in range(1, NX)]
    peers += [dev(z, y, 1 - c, x)]
    for p in peers:
        pl.semaphore_signal(bar, inc=1, device_id=p, device_id_type=pl.DeviceIdType.MESH)
    pl.semaphore_wait(bar, len(peers))

    for way in range(2):
        z1(0, way, 1).start()
    for d in range(1, NY):
        y2(0, d).start()
    own_w = pltpu.make_async_copy(w, wbuf.at[x], wls)
    own_w.start()
    for i in range(len(WCH)):
        for way in range(2):
            w1(way, i).start()

    def need(dest, base_at, origins):
        b = pb[dest]
        g = [gates[b, e] for e in range(TOPK)] + [gates[63 - b, e] for e in range(TOPK)]
        for i, origin in enumerate(origins):
            late = 63 - pb[origin]
            hit = g[0] == late
            for v in g[1:]:
                hit = hit | (v == late)
            bits[base_at + i] = jnp.where(hit, 1, 0)

    def need1(d, _):
        need(z * 4 + mod(y + d, NY), d * 8, [mod(z + r, NZ) * 4 + y for r in range(NZ)])
        return 0

    def need2(r, _):
        need(mod(z + r, NZ) * 4 + y, 32 + r * 4, [z * 4 + mod(y + j, NY) for j in range(NY)])
        return 0

    lax.fori_loop(0, NY, need1, 0)

    def put1(k, r):
        z0 = mod(z + r, NZ)
        if r == 0:
            a, b = kvin[k, 0, 0:R1], kvin[k, 1, 0:R1]
        else:
            a, b = col[k][z0, 0], col[k][z0, 1]
        for d in range(1, NY):
            st1[k][r, d - 1] = jnp.where(bits[d * 8 + r] > 0, b, a)
            y1(k, r, d).start()
        if r != 0:
            sel[k][z0 * 4 + y, pl.ds(base, R1)] = jnp.where(bits[r] > 0, b, a)

    def put2(k, j):
        yo = mod(y + j, NY)

        def one(r, _):
            if j == 0:
                a, b = kvin[k, 0, R1:HALF], kvin[k, 1, R1:HALF]
            else:
                a, b = row[k][yo, 0], row[k][yo, 1]
            st2[k][r, j] = jnp.where(bits[32 + r * 4 + j] > 0, b, a)
            z2(k, r, j).start()
            return 0

        lax.fori_loop(1, NZ, one, 0)
        if j != 0:
            a, b = row[k][yo, 0], row[k][yo, 1]
            sel[k][z * 4 + yo, pl.ds(base + R1, R2)] = jnp.where(bits[32 + j] > 0, b, a)

    def put_own(k):
        sel[k][me, pl.ds(base, HALF)] = kvin[k, 0]
        sel[k][32, pl.ds(base, HALF)] = kvin[k, 1]
        sib_own(k).start()

    def ring(k, hop):
        for way in range(2):
            z1(k, way, hop).wait_recv()
            if hop < 4:
                z1(k, way, hop + 1).start()
        for r in ((NZ - hop, hop) if hop < 4 else (4,)):
            put1(k, r)

    def rows_in(k):
        for d in range(1, NY):
            y2(k, d).wait_recv()
        for j in range(1, NY):
            put2(k, j)

    def collect(k, r):
        for d in range(1, NY):
            y1(k, r, d).wait_recv()
        if r != 0:
            for j in range(NY):
                z2(k, NZ - r, j).wait_recv()
        sib(k, r).start()

    put1(0, 0)
    lax.fori_loop(0, NZ, need2, 0)
    put_own(0)
    ring(0, 1)
    put2(0, 0)
    ring(0, 2)
    rows_in(0)
    ring(0, 3)
    ring(0, 4)

    own_early = pb[me]
    ent = [gates[own_early, e] for e in range(TOPK)] + [gates[63 - own_early, e] for e in range(TOPK)]

    def find(p, at):
        b = pb[p]
        return tuple(jnp.where((g == b) | (g == 63 - b), p, v) for g, v in zip(ent, at))

    at = lax.fori_loop(0, NZ * NY, find, tuple(jnp.int32(0) for _ in ent))
    for i, (g, v) in enumerate(zip(ent, at)):
        slots[i] = jnp.where(g == 63 - own_early, 32, jnp.where(g < 0, me, v))
        valid[i] = jnp.where(g >= 0, 1, 0)

    put_own(1)
    for way in range(2):
        z1(1, way, 1).start()
    for d in range(1, NY):
        y2(1, d).start()
    put1(1, 0)
    for r in (0, 1, 7, 2, 6, 3, 5, 4):
        collect(0, r)
    ring(1, 1)
    put2(1, 0)
    for r in range(NZ):
        sib(0, r).wait_recv()
    sib_own(0).wait_recv()

    def unit(u, _):
        di, hp = lax.div(u, jnp.int32(2)), mod(u, 2)
        d = jnp.where(di == 0, 2, jnp.where(di == 1, 1, jnp.where(di == 2, 3, 0)))
        dest = mod(x + d, NX)
        side8 = lax.div(dest, jnp.int32(2)) * 8
        qr = q[pl.ds(pl.multiple_of(dest * 128, 128), 128), pl.ds(pl.multiple_of(hp * 256, 256), 256)]
        qs = jnp.concatenate([qr[:, 0:128], qr[:, 128:256]], axis=0)
        hrow = pl.multiple_of(hp * 256, 256)
        qpos = mod(lax.broadcasted_iota(jnp.int32, (256, 128), 0), 128) + c * HALF + mod(dest, 2) * 128
        lane = lax.broadcasted_iota(jnp.int32, (256, 128), 1)
        m = jnp.full((256, 128), NEG, f32)
        for e in range(TOPK):
            sc = dot_nt(qs, sel_k[slots[side8 + e]])
            best = None
            for t in range(4):
                part = sc[:, t * 128:(t + 1) * 128]
                if e == 0:
                    part = jnp.where(lane + t * 128 <= qpos, part, NEG)
                s_acc[e, t] = part
                best = part if best is None else jnp.maximum(best, part)
            if e:
                best = jnp.where(valid[side8 + e] > 0, best, NEG)
            m = jnp.maximum(m, best)
        m = jnp.max(m, axis=1, keepdims=True)
        total = jnp.zeros((256, 128), f32)
        for e in range(TOPK):
            peak = m if e == 0 else jnp.where(valid[side8 + e] > 0, m, BIG)
            for t in range(4):
                p = jnp.exp2((s_acc[e, t] - peak) * SCALE)
                total = total + p
                p_buf[di, e, pl.ds(hrow, 256), t * 128:(t + 1) * 128] = p.astype(bf16)
        l_buf[di, pl.ds(hrow, 256)] = total
        return 0

    lax.fori_loop(0, 2, unit, 0)
    ring(1, 2)
    rows_in(1)
    lax.fori_loop(2, 4, unit, 0)
    ring(1, 3)
    ring(1, 4)
    lax.fori_loop(4, 8, unit, 0)
    for r in (0, 1, 7, 2, 6, 3, 5, 4):
        collect(1, r)
    for r in range(NZ):
        sib(1, r).wait_recv()
    sib_own(1).wait_recv()

    for i in range(len(WCH)):
        for way in range(2):
            w1(way, i).wait_recv()
            w2(way, i).start()
        wsib(1, i).start()
        wsib(3, i).start()

    for di, d in enumerate(ORDER):
        dest = mod(x + d, NX)
        side8 = lax.div(dest, jnp.int32(2)) * 8
        acc = jnp.zeros((512, 128), f32)
        for e in range(TOPK):
            acc = acc + jnp.dot(p_buf[di, e], sel_v[slots[side8 + e]], preferred_element_type=f32)
        out = (acc / jnp.sum(l_buf[di], axis=1, keepdims=True)).astype(bf16)
        for h in range(4):
            part = out[h * 128:(h + 1) * 128]
            if d == 0:
                attg[x, :, h * 128:(h + 1) * 128] = part
            else:
                att_s[d - 1, :, h * 128:(h + 1) * 128] = part
        if d:
            send_att(d).start()

    for i in range(len(WCH)):
        for way in range(2):
            w2(way, i).wait_recv()
        wsib(2, i).start()
    for i in range(len(WCH)):
        for d in range(1, NX):
            wsib(d, i).wait_recv()
    own_w.wait()
    for d in range(1, NX):
        send_att(d).wait_recv()

    def project(n, _):
        cols = pl.ds(pl.multiple_of(n * 512, 512), 512)
        acc = jnp.dot(attg[0], wbuf[0, :, cols], preferred_element_type=f32)
        for i in range(1, NX):
            acc = acc + jnp.dot(attg[i], wbuf[i, :, cols], preferred_element_type=f32)
        o[:, cols] = acc.astype(bf16)
        return 0

    lax.fori_loop(0, 8, project, 0)

    for k in range(2):
        for way in range(2):
            for hop in range(1, 5):
                z1(k, way, hop).wait_send()
        for d in range(1, NY):
            y2(k, d).wait_send()

        def done1(r, _, k=k):
            for d in range(1, NY):
                y1(k, r, d).wait_send()
            sib(k, r).wait_send()
            return 0

        def done2(r, _, k=k):
            for j in range(NY):
                z2(k, r, j).wait_send()
            return 0

        lax.fori_loop(0, NZ, done1, 0)
        lax.fori_loop(1, NZ, done2, 0)
        sib_own(k).wait_send()
    for i in range(len(WCH)):
        for way in range(2):
            w1(way, i).wait_send()
            w2(way, i).wait_send()
        for d in range(1, NX):
            wsib(d, i).wait_send()
    for d in range(1, NX):
        send_att(d).wait_send()


def body(queries, keyval, gates, pair_block, out_weight):
    kv = keyval.reshape(2, 2, HALF, HD)
    vmem, smem = pl.BlockSpec(memory_space=pltpu.VMEM), pl.BlockSpec(memory_space=pltpu.SMEM)
    n = len(WCH)
    dma = pltpu.SemaphoreType.DMA
    scratch = (
        [pltpu.VMEM((33, 512, HD), bf16)] * 2
        + [pltpu.VMEM((NZ, 2, R1, HD), bf16)] * 2
        + [pltpu.VMEM((NY, 2, R2, HD), bf16)] * 2
        + [pltpu.VMEM((NZ, 3, R1, HD), bf16)] * 2
        + [pltpu.VMEM((NZ, NY, R2, HD), bf16)] * 2
        + [
            pltpu.VMEM((NX, 512, 4096), bf16),
            pltpu.VMEM((TOPK, 4, 256, 128), f32),
            pltpu.VMEM((NX, TOPK, 512, 512), bf16),
            pltpu.VMEM((NX, 512, 128), f32),
            pltpu.VMEM((3, 128, 512), bf16),
            pltpu.VMEM((NX, 128, 512), bf16),
            pltpu.SMEM((64,), jnp.int32),
            pltpu.SMEM((16,), jnp.int32),
            pltpu.SMEM((16,), jnp.int32),
        ]
        + [dma((2, 2, 4))] * 2
        + [dma((2, 3))] * 2
        + [dma((2, NZ, 3))] * 2
        + [dma((2, NZ, NY))] * 2
        + [dma((2, 9))] * 2
        + [dma((2, n))] * 4
        + [dma((3, n))] * 2
        + [dma((3,))] * 2
        + [dma]
    )
    return pl.pallas_call(
        kernel,
        out_shape=jax.ShapeDtypeStruct((128, 4096), bf16),
        in_specs=[smem, smem, vmem, vmem, pl.BlockSpec(memory_space=pl.ANY)],
        out_specs=vmem,
        scratch_shapes=scratch,
        name="block_attention",
        cost_estimate=pl.CostEstimate(flops=6 * 2**30, bytes_accessed=8 * 2**20, transcendentals=8 * 2**20),
        compiler_params=pltpu.CompilerParams(
            collective_id=0, has_side_effects=True, vmem_limit_bytes=62 * 2**20),
    )(gates, pair_block, queries, kv, out_weight)


def solution(mesh):
    placed = (P("seq", "head"), P(None, "seq", "head"), P(), P(), P("head", None))
    return jax.shard_map(
        body, mesh=mesh, in_specs=placed, out_specs=P(("seq", "head"), None), check_vma=False
    )
```

time: 253 us -> 108 us (0.43)
  waiting for transfers between devices: 176 us -> 0 us
  Pallas kernels: 0 us -> 105 us
  matrix products: 23.6 us -> 0 us
  other arithmetic: 23.3 us -> 0 us
  between operations: 14.3 us -> 0.01 us
  local copies, waits for them, and re-layouts: 14.9 us -> 3.67 us
    pallas_call x0 -> x1, Pallas kernels: none -> 105 us  [body(): pl.pallas_call(kernel, out_shape=jax.ShapeDtypeStruct((128, 4096), bf16),...]
    all_gather x1 -> x0, waiting for transfers between devices: 95.6 us -> none  [body(): gathered = lax.all_gather(keyval, 'seq', axis=1, tiled=True)]
    reduce_scatter x1 -> x0, waiting for transfers between devices: 79.8 us -> none  [body(): lax.psum_scatter(jnp.dot(attended, out_weight, preferred_element_type=jnp...]
    dot_general x5 -> x0, matrix products: 23.6 us -> none  [the longest x2 11.3 us: attend(): jnp.einsum('kgql,lkd->qkgd', rounded, picked[1], preferred_element_type=j...]
    reduce_sum x5 -> x0, other arithmetic: 11.5 us -> none  [the longest x2 8.54 us: attend(): row_total = jnp.sum(weights, axis=-1)]
    gather x2 -> x0, local copies, waits for them, and re-layouts: 11.2 us -> none  [body(): picked = jnp.take(kv_table, piece_index.reshape(-1), axis=1)]
    and x2 -> x0, other arithmetic: 4.33 us -> none  [the longest x1 4.32 us: attend(): (listed >= 0)[None, :]]
    select_n x3 -> x0, other arithmetic: 3.24 us -> none  [the longest x2 3.24 us: body(): picked = jnp.take(kv_table, piece_index.reshape(-1), axis=1)]
  transfers between devices with their start and end apart: 2 -> 0, of which waited for: 2 -> 0; matrix products, arithmetic and copies ran while one was open for 4% -> 0% of each run, Pallas kernels for 0% -> 0%
where the time goes in v1:
time: 108 us
  Pallas kernels  105 us (97%)
  local copies, waits for them, and re-layouts  3.67 us (3%)
    pallas_call x1, Pallas kernels, body(): pl.pallas_call(kernel, out_shape=jax.ShapeDtypeStruct((128, 4096), bf16),...  105 us
    unnamed x2, local copies, waits for them, and re-layouts  3.67 us

profile of v1, /device:TPU:1, one launch (start us, length us, event | category | flops | bytes accessed | tf_op | source)
XLA Modules:
  0.0 108.3 jit_solution(5117625911734631418)
XLA Ops:
  0.0 1.4 %copy.6.gates = s32[64,8]{1,0:T(8,128)} copy(s32[64,8]{0,1:T(8,128)} %param.7) | data formatting | bytes 4096 | tf_op args[2]
  1.4 104.6 %block_attention.1 = bf16[128,4096]{1,0:T(8,128)(2,1)} custom-call(s32[64,8]{1,0:T(8,128)} %copy.6.gates, s32[32]{0:T(128)} %pb.1, bf16[512,512]{1,0:T(8,128)(2,1)} %q.1, bf16[2,2,256,128]{3,2,1,0:T(8,128)(2,1)} %bitcast.1, bf16[512,4096]{1,0:T(8,128)(2,1)} %w.1), custom_call_target="tpu_custom_call" | custom-call | flops 6442450944 | bytes 8388608 | tf_op jit(solution)/shard_map/block_attention/pallas_call | solution.py:387
  106.0 2.3 %copy.8 = bf16[128,4096]{1,0:T(8,128)(2,1)} copy(bf16[128,4096]{1,0:T(8,128)(2,1)} %block_attention.1) | data formatting | bytes 2097152

commit v2 on v1

v2 whole, which is shorter than its diff:
```python
import jax
import jax.numpy as jnp
from jax import lax
from jax.experimental import pallas as pl
from jax.experimental.pallas import tpu as pltpu
from jax.sharding import PartitionSpec as P

HD = 128
TOPK = 8
HALF = 256
NZ, NY, NX = 8, 4, 4
SCALE = 1.4426950408889634 / 128**0.5
NEG = -1e30
BIG = 1e30
WS = ((0, 384), (384, 384))
WP = 768
WD = ((1536, 512),)
NS, NW = len(WS), len(WS) + len(WD)
ORDER = (2, 1, 3, 0)
STEPS = (
    ("R", 0, 0), ("W", 0), ("N1",), ("P", 0, 0), ("R", 1, 0), ("O", 0), ("O", 1), ("R", 0, 1), ("P", 0, 1),
    ("R", 1, 1), ("W", 1), ("R", 0, 2), ("P", 0, 2), ("R", 1, 2), ("R", 0, 3), ("P", 0, 3), ("X", 0), ("R", 1, 3),
    ("R", 0, 4), ("P", 0, 4), ("R", 1, 4), ("F",), ("C", 0, 0), ("C", 0, 1), ("C", 0, 7), ("X", 1), ("L", 0),
    ("W", 2), ("H", 0), ("D", 0, 2), ("D", 0, 6), ("P", 1, 0), ("C", 0, 2), ("C", 0, 6), ("D", 0, 3), ("D", 0, 5),
    ("P", 1, 1), ("C", 0, 3), ("C", 0, 5), ("D", 0, 4), ("P", 1, 2), ("C", 0, 4), ("S", 0), ("L", 1), ("H", 1),
    ("U", 0, 2), ("P", 1, 3), ("U", 2, 4), ("P", 1, 4), ("C", 1, 0), ("U", 4, 6), ("C", 1, 1), ("C", 1, 7),
    ("U", 6, 8), ("X", 2), ("C", 1, 2), ("C", 1, 6), ("C", 1, 3), ("C", 1, 5), ("C", 1, 4), ("G", 0), ("S", 1),
    ("V",), ("G", 1), ("L", 2), ("I",),
)
f32, bf16 = jnp.float32, jnp.bfloat16


def mod(a, n):
    return lax.rem(a, jnp.int32(n))


def dot_nt(a, b):
    return lax.dot_general(a, b, (((1,), (1,)), ((), ())), preferred_element_type=f32)


def kernel(gates, pb, q, kvin, w, o, sel_k, sel_v, col_k, col_v, st1_k, st1_v,
           wbuf, s_acc, p_buf, l_buf, att_s, attg, bits, slots, valid,
           z1s, z1r, y1s, y1r, sbs, sbr, wss, wsr, wfs, wfr, wbs, wbr, shs, shr, ats, atr, wls):
    s = lax.axis_index("seq").astype(jnp.int32)
    x = lax.axis_index("head").astype(jnp.int32)
    z = lax.div(s, jnp.int32(8))
    y = mod(lax.div(s, jnp.int32(2)), 4)
    c = mod(s, 2)
    me = z * 4 + y
    sel, col, st1 = (sel_k, sel_v), (col_k, col_v), (st1_k, st1_v)
    base = pl.multiple_of(c * HALF, HALF)

    def dev(zz, yy, cc, xx):
        return ((zz * 4 + yy) * 2 + cc, xx)

    def remote(src, dst, ssem, rsem, device):
        return pltpu.make_async_remote_copy(
            src_ref=src, dst_ref=dst, send_sem=ssem, recv_sem=rsem,
            device_id=device, device_id_type=pl.DeviceIdType.MESH)

    def z1(k, way, hop):
        step = 1 if way == 0 else NZ - 1
        zo = mod(z + (NZ - step) * (hop - 1), NZ)
        lo, n = (0, HALF) if hop < 4 else ((0, HALF // 2) if way == 0 else (HALF // 2, HALF // 2))
        src = kvin.at[k, :, 0:HALF] if hop == 1 else col[k].at[zo, :, lo:lo + n]
        return remote(src, col[k].at[zo, :, lo:lo + n], z1s.at[k, way, hop - 1], z1r.at[k, way, hop - 1],
                      dev(mod(z + step, NZ), y, c, x))

    def y1(k, r, d):
        slot = mod(z + r, NZ) * 4 + y
        return remote(st1[k].at[r, d - 1], sel[k].at[slot, pl.ds(base, HALF)], y1s.at[k, r, d - 1],
                      y1r.at[k, r, d - 1], dev(z, mod(y + d, NY), c, x))

    def sib(k, r):
        at = sel[k].at[pl.ds(mod(z + r, NZ) * 4, 4), pl.ds(base, HALF)]
        return remote(at, at, sbs.at[k, r], sbr.at[k, r], dev(z, y, 1 - c, x))

    def sib_own(k):
        at = sel[k].at[32, pl.ds(base, HALF)]
        return remote(at, at, sbs.at[k, 8], sbr.at[k, 8], dev(z, y, 1 - c, x))

    def wcols(i):
        if NS <= i < NW:
            off, n = WD[i - NS]
        else:
            off, n = WS[i % NW]
            off = off + mod(z + (0 if i < NS else 1), 2) * WP
        return pl.ds(pl.multiple_of(c * 2048 + off, 128), n)

    def w1(way, i):
        step = 1 if way == 0 else NX - 1
        return remote(w.at[:, wcols(i)], wbuf.at[x, :, wcols(i)], wss.at[way, i], wsr.at[way, i],
                      dev(z, y, c, mod(x + step, NX)))

    def w2(way, i):
        step = 1 if way == 0 else NX - 1
        at = wbuf.at[mod(x + NX - step, NX), way * 256:way * 256 + 256, wcols(i)]
        return remote(at, at, wfs.at[way, i], wfr.at[way, i], dev(z, y, c, mod(x + step, NX)))

    def wsib(d, i):
        at = wbuf.at[mod(x + d, NX), :, wcols(i)]
        return remote(at, at, wbs.at[d - 1, i], wbr.at[d - 1, i], dev(z, y, 1 - c, x))

    def share(i, way, d):
        at = wbuf.at[mod(x + d, NX), way * 256:way * 256 + 256, wcols(i)]
        return remote(at, at, shs.at[i, way, d - 1], shr.at[i, way, d - 1],
                      dev(mod(z + (1 if way == 0 else NZ - 1), NZ), y, c, x))

    def send_att(d):
        return remote(att_s.at[d - 1], attg.at[x], ats.at[d - 1], atr.at[d - 1], dev(z, y, c, mod(x + d, NX)))

    own_w = pltpu.make_async_copy(w, wbuf.at[x], wls)
    own_w.start()
    bar = pltpu.get_barrier_semaphore()
    peers = [dev(mod(z + r, NZ), y, c, x) for r in (1, NZ - 1)]
    peers += [dev(z, mod(y + d, NY), c, x) for d in range(1, NY)]
    peers += [dev(z, y, c, mod(x + d, NX)) for d in range(1, NX)]
    peers += [dev(z, y, 1 - c, x)]
    for p in peers:
        pl.semaphore_signal(bar, inc=1, device_id=p, device_id_type=pl.DeviceIdType.MESH)
    pl.semaphore_wait(bar, len(peers))

    def need(dest, base_at, origins):
        b = pb[dest]
        g = [gates[e, b] for e in range(TOPK)] + [gates[e, 63 - b] for e in range(TOPK)]
        for i, origin in enumerate(origins):
            late = 63 - pb[origin]
            hit = g[0] == late
            for v in g[1:]:
                hit = hit | (v == late)
            bits[base_at + i] = jnp.where(hit, 1, 0)

    def need1(d, _):
        need(z * 4 + mod(y + d, NY), d * 8, [mod(z + r, NZ) * 4 + y for r in range(NZ)])
        return 0

    def put1(k, r):
        z0 = mod(z + r, NZ)
        if r == 0:
            a, b = kvin[k, 0, 0:HALF], kvin[k, 1, 0:HALF]
        else:
            a, b = col[k][z0, 0], col[k][z0, 1]
        for d in range(1, NY):
            st1[k][r, d - 1] = jnp.where(bits[d * 8 + r] > 0, b, a)
            y1(k, r, d).start()
        if r != 0:
            sel[k][z0 * 4 + y, pl.ds(base, HALF)] = jnp.where(bits[r] > 0, b, a)

    def put_own(k):
        sel[k][me, pl.ds(base, HALF)] = kvin[k, 0]
        sel[k][32, pl.ds(base, HALF)] = kvin[k, 1]
        sib_own(k).start()

    def ring(k, hop):
        for way in range(2):
            if hop:
                z1(k, way, hop).wait_recv()
            if hop < 4:
                z1(k, way, hop + 1).start()

    def rounds(k, hop):
        for r in {0: (0,), 4: (4,)}.get(hop, (NZ - hop, hop)):
            put1(k, r)

    def collect(k, r):
        for d in range(1, NY):
            y1(k, r, d).wait_recv()
        sib(k, r).start()

    drained = set()

    def drain(k, r):
        drained.add((k, r))
        for d in range(1, NY):
            y1(k, r, d).wait_send()

    def sib_in(k):
        for r in range(NZ):
            sib(k, r).wait_recv()
        sib_own(k).wait_recv()

    def find_slots():
        own_early = pb[me]
        ent = [gates[e, own_early] for e in range(TOPK)] + [gates[e, 63 - own_early] for e in range(TOPK)]

        def find(p, at):
            b = pb[p]
            return tuple(jnp.where((g == b) | (g == 63 - b), p, v) for g, v in zip(ent, at))

        at = lax.fori_loop(0, NZ * NY, find, tuple(jnp.int32(0) for _ in ent))
        for i, (g, v) in enumerate(zip(ent, at)):
            slots[i] = jnp.where(g == 63 - own_early, 32, jnp.where(g < 0, me, v))
            valid[i] = jnp.where(g >= 0, 1, 0)

    def unit(u, _):
        di, hp = lax.div(u, jnp.int32(2)), mod(u, 2)
        d = jnp.where(di == 0, 2, jnp.where(di == 1, 1, jnp.where(di == 2, 3, 0)))
        dest = mod(x + d, NX)
        side8 = lax.div(dest, jnp.int32(2)) * 8
        qr = q[pl.ds(pl.multiple_of(dest * 128, 128), 128), pl.ds(pl.multiple_of(hp * 256, 256), 256)]
        qs = jnp.concatenate([qr[:, 0:128], qr[:, 128:256]], axis=0)
        hrow = pl.multiple_of(hp * 256, 256)
        qpos = mod(lax.broadcasted_iota(jnp.int32, (256, 128), 0), 128) + c * HALF + mod(dest, 2) * 128
        lane = lax.broadcasted_iota(jnp.int32, (256, 128), 1)
        m = jnp.full((256, 128), NEG, f32)
        for e in range(TOPK):
            sc = dot_nt(qs, sel_k[slots[side8 + e]])
            best = None
            for t in range(4):
                part = sc[:, t * 128:(t + 1) * 128]
                if e == 0:
                    part = jnp.where(lane + t * 128 <= qpos, part, NEG)
                s_acc[e, t] = part
                best = part if best is None else jnp.maximum(best, part)
            if e:
                best = jnp.where(valid[side8 + e] > 0, best, NEG)
            m = jnp.maximum(m, best)
        m = jnp.max(m, axis=1, keepdims=True)
        total = jnp.zeros((256, 128), f32)
        for e in range(TOPK):
            peak = m if e == 0 else jnp.where(valid[side8 + e] > 0, m, BIG)
            for t in range(4):
                p = jnp.exp2((s_acc[e, t] - peak) * SCALE)
                total = total + p
                p_buf[di, e, pl.ds(hrow, 256), t * 128:(t + 1) * 128] = p.astype(bf16)
        l_buf[di, pl.ds(hrow, 256)] = total
        return 0

    def w_start(i):
        for way in range(2):
            w1(way, i).start()

    def w_forward(i):
        for way in range(2):
            w1(way, i).wait_recv()
            w2(way, i).start()
        wsib(1, i).start()
        wsib(3, i).start()

    def w_last(i):
        for way in range(2):
            w2(way, i).wait_recv()
        wsib(2, i).start()

    def w_share(i):
        for d in range(1, NX):
            for way in range(2):
                share(i, way, d).start()

    def w_shared(i):
        for d in range(1, NX):
            for way in range(2):
                share(i, way, d).wait_recv()
            wsib(d, NW + i).start()

    def w_in():
        for i in range(NW + NS):
            for d in range(1, NX):
                wsib(d, i).wait_recv()

    def values():
        for di, d in enumerate(ORDER):
            dest = mod(x + d, NX)
            side8 = lax.div(dest, jnp.int32(2)) * 8
            acc = jnp.zeros((512, 128), f32)
            for e in range(TOPK):
                acc = acc + jnp.dot(p_buf[di, e], sel_v[slots[side8 + e]], preferred_element_type=f32)
            out = (acc / jnp.sum(l_buf[di], axis=1, keepdims=True)).astype(bf16)
            for h in range(4):
                part = out[h * 128:(h + 1) * 128]
                if d == 0:
                    attg[x, :, h * 128:(h + 1) * 128] = part
                else:
                    att_s[d - 1, :, h * 128:(h + 1) * 128] = part
            if d:
                send_att(d).start()

    acts = {
        "N1": lambda: lax.fori_loop(0, NY, need1, 0), "F": find_slots, "O": put_own, "R": ring, "P": rounds, "C": collect,
        "S": sib_in, "U": lambda a, b: lax.fori_loop(a, b, unit, 0), "W": w_start, "X": w_forward,
        "V": None,
    }
    acts["D"] = drain
    acts["V"] = values
    acts["L"] = w_last
    acts["I"] = w_in
    acts["H"] = w_share
    acts["G"] = w_shared
    for step in STEPS:
        acts[step[0]](*step[1:])
    started = {a[0] for a in STEPS}
    has = {a[:2] for a in STEPS}
    own_w.wait()
    for d in range(1, NX if "V" in started else 0):
        send_att(d).wait_recv()

    def project(n, _):
        cols = pl.ds(pl.multiple_of(n * 512, 512), 512)
        acc = jnp.dot(attg[0], wbuf[0, :, cols], preferred_element_type=f32)
        for i in range(1, NX):
            acc = acc + jnp.dot(attg[i], wbuf[i, :, cols], preferred_element_type=f32)
        o[:, cols] = acc.astype(bf16)
        return 0

    lax.fori_loop(0, 8, project, 0)

    for k in range(2):
        if ("R", k) in has:
            for way in range(2):
                for hop in range(1, 5):
                    z1(k, way, hop).wait_send()
        for r in range(NZ):
            if ("P", k) in has and (k, r) not in drained:
                drain(k, r)
            if ("C", k) in has:
                sib(k, r).wait_send()
        if ("O", k) in has:
            sib_own(k).wait_send()
    if "W" in started:
        for i in range(NW):
            for way in range(2):
                w1(way, i).wait_send()
                w2(way, i).wait_send()
        for i in range(NW + NS):
            for d in range(1, NX):
                wsib(d, i).wait_send()
        for i in range(NS):
            for d in range(1, NX):
                for way in range(2):
                    share(i, way, d).wait_send()
    for d in range(1, NX if "V" in started else 0):
        send_att(d).wait_send()


def body(queries, keyval, gates, pair_block, out_weight):
    kv = keyval.reshape(2, 2, HALF, HD)
    vmem, smem = pl.BlockSpec(memory_space=pltpu.VMEM), pl.BlockSpec(memory_space=pltpu.SMEM)
    dma = pltpu.SemaphoreType.DMA
    scratch = (
        [pltpu.VMEM((33, 512, HD), bf16)] * 2
        + [pltpu.VMEM((NZ, 2, HALF, HD), bf16)] * 2
        + [pltpu.VMEM((NZ, 3, HALF, HD), bf16)] * 2
        + [
            pltpu.VMEM((NX, 512, 4096), bf16),
            pltpu.VMEM((TOPK, 4, 256, 128), f32),
            pltpu.VMEM((NX, TOPK, 512, 512), bf16),
            pltpu.VMEM((NX, 512, 128), f32),
            pltpu.VMEM((3, 128, 512), bf16),
            pltpu.VMEM((NX, 128, 512), bf16),
            pltpu.SMEM((64,), jnp.int32),
            pltpu.SMEM((16,), jnp.int32),
            pltpu.SMEM((16,), jnp.int32),
        ]
        + [dma((2, 2, 4))] * 2
        + [dma((2, NZ, 3))] * 2
        + [dma((2, 9))] * 2
        + [dma((2, NW))] * 4
        + [dma((3, NW + NS))] * 2
        + [dma((NS, 2, 3))] * 2
        + [dma((3,))] * 2
        + [dma]
    )
    return pl.pallas_call(
        kernel,
        out_shape=jax.ShapeDtypeStruct((128, 4096), bf16),
        in_specs=[smem, smem, vmem, vmem, pl.BlockSpec(memory_space=pl.ANY)],
        out_specs=vmem,
        scratch_shapes=scratch,
        name="block_attention",
        cost_estimate=pl.CostEstimate(flops=6 * 2**30, bytes_accessed=8 * 2**20, transcendentals=8 * 2**20),
        compiler_params=pltpu.CompilerParams(
            collective_id=0, has_side_effects=True, vmem_limit_bytes=62 * 2**20),
    )(gates.T, pair_block, queries, kv, out_weight)


def solution(mesh):
    placed = (P("seq", "head"), P(None, "seq", "head"), P(), P(), P("head", None))
    return jax.shard_map(
        body, mesh=mesh, in_specs=placed, out_specs=P(("seq", "head"), None), check_vma=False
    )
```

time: 108 us -> 82.2 us (0.76)
  Pallas kernels: 105 us -> 79.8 us
  local copies, waits for them, and re-layouts: 3.67 us -> 2.29 us
    pallas_call x1, Pallas kernels: 105 us -> 79.8 us  [body(): pl.pallas_call(kernel, out_shape=jax.ShapeDtypeStruct((128, 4096), bf16),...]
    unnamed x2 -> x1, local copies, waits for them, and re-layouts: 3.67 us -> 2.29 us
where the time goes in v2:
time: 82.2 us; the launch traced here: 82.1 us
  Pallas kernels  79.8 us (97%)
  local copies, waits for them, and re-layouts  2.29 us (3%)
    pallas_call x1, Pallas kernels, body(): pl.pallas_call(kernel, out_shape=jax.ShapeDtypeStruct((128, 4096), bf16),...  79.8 us
    unnamed x1, local copies, waits for them, and re-layouts  2.29 us

profile of v2, /device:TPU:1, one launch (start us, length us, event | category | flops | bytes accessed | tf_op | source)
XLA Modules:
  0.0 82.1 jit_solution(322459987769015734)
XLA Ops:
  0.0 79.8 %block_attention.1 = bf16[128,4096]{1,0:T(8,128)(2,1)} custom-call(s32[8,64]{1,0:T(8,128)} %bitcast.3, s32[32]{0:T(128)} %pb.1, bf16[512,512]{1,0:T(8,128)(2,1)} %q.1, bf16[2,2,256,128]{3,2,1,0:T(8,128)(2,1)} %bitcast.2, bf16[512,4096]{1,0:T(8,128)(2,1)} %w.1), custom_call_target="tpu_custom_call" | custom-call | flops 6442450944 | bytes 8388608 | tf_op jit(solution)/shard_map/block_attention/pallas_call | solution.py:363
  79.8 2.3 %copy.7 = bf16[128,4096]{1,0:T(8,128)(2,1)} copy(bf16[128,4096]{1,0:T(8,128)(2,1)} %block_attention.1) | data formatting | bytes 2097152

commit v3 on v2

--- a/solution.py
+++ b/solution.py
@@ -18,14 +18,13 @@
 NS, NW = len(WS), len(WS) + len(WD)
 ORDER = (2, 1, 3, 0)
 STEPS = (
-    ("R", 0, 0), ("W", 0), ("N1",), ("P", 0, 0), ("R", 1, 0), ("O", 0), ("O", 1), ("R", 0, 1), ("P", 0, 1),
-    ("R", 1, 1), ("W", 1), ("R", 0, 2), ("P", 0, 2), ("R", 1, 2), ("R", 0, 3), ("P", 0, 3), ("X", 0), ("R", 1, 3),
-    ("R", 0, 4), ("P", 0, 4), ("R", 1, 4), ("F",), ("C", 0, 0), ("C", 0, 1), ("C", 0, 7), ("X", 1), ("L", 0),
-    ("W", 2), ("H", 0), ("D", 0, 2), ("D", 0, 6), ("P", 1, 0), ("C", 0, 2), ("C", 0, 6), ("D", 0, 3), ("D", 0, 5),
-    ("P", 1, 1), ("C", 0, 3), ("C", 0, 5), ("D", 0, 4), ("P", 1, 2), ("C", 0, 4), ("S", 0), ("L", 1), ("H", 1),
-    ("U", 0, 2), ("P", 1, 3), ("U", 2, 4), ("P", 1, 4), ("C", 1, 0), ("U", 4, 6), ("C", 1, 1), ("C", 1, 7),
-    ("U", 6, 8), ("X", 2), ("C", 1, 2), ("C", 1, 6), ("C", 1, 3), ("C", 1, 5), ("C", 1, 4), ("G", 0), ("S", 1),
-    ("V",), ("G", 1), ("L", 2), ("I",),
+    ("N1",), ("F",), ("B",), ("R", 0, 0), ("W", 0), ("P", 0, 0), ("R", 1, 0), ("O", 0), ("O", 1), ("R", 0, 1),
+    ("P", 0, 1), ("R", 1, 1), ("W", 1), ("R", 0, 2), ("P", 0, 2), ("R", 1, 2), ("R", 0, 3), ("P", 0, 3), ("X", 0),
+    ("R", 1, 3), ("R", 0, 4), ("P", 0, 4), ("R", 1, 4), ("P", 1, 0), ("C", 0, 0), ("C", 0, 1), ("C", 0, 7),
+    ("X", 1), ("L", 0), ("W", 2), ("H", 0), ("P", 1, 1), ("P", 1, 2), ("C", 0, 2), ("C", 0, 6), ("P", 1, 3),
+    ("P", 1, 4), ("L", 1), ("H", 1), ("C", 0, 3), ("C", 0, 5), ("C", 0, 4), ("S", 0), ("U", 0, 4), ("C", 1, 0),
+    ("C", 1, 1), ("C", 1, 7), ("U", 4, 8), ("X", 2), ("C", 1, 2), ("C", 1, 6), ("C", 1, 3), ("C", 1, 5),
+    ("C", 1, 4), ("G", 0), ("S", 1), ("V",), ("G", 1), ("L", 2), ("J", 0), ("J", 1), ("J", 3), ("J", 2),
 )
 f32, bf16 = jnp.float32, jnp.bfloat16
 
@@ -118,7 +117,6 @@
     peers += [dev(z, y, 1 - c, x)]
     for p in peers:
         pl.semaphore_signal(bar, inc=1, device_id=p, device_id_type=pl.DeviceIdType.MESH)
-    pl.semaphore_wait(bar, len(peers))
 
     def need(dest, base_at, origins):
         b = pb[dest]
@@ -253,11 +251,6 @@
                 share(i, way, d).wait_recv()
             wsib(d, NW + i).start()
 
-    def w_in():
-        for i in range(NW + NS):
-            for d in range(1, NX):
-                wsib(d, i).wait_recv()
-
     def values():
         for di, d in enumerate(ORDER):
             dest = mod(x + d, NX)
@@ -275,35 +268,42 @@
             if d:
                 send_att(d).start()
 
+    def project(d):
+        at = mod(x + d, NX)
+        if d:
+            send_att(NX - d).wait_recv()
+            for i in range(NW + NS):
+                wsib(d, i).wait_recv()
+        else:
+            own_w.wait()
+        left = attg[at]
+        for n in range(8):
+            acc = jnp.dot(left, wbuf[at, :, n * 512:(n + 1) * 512], preferred_element_type=f32)
+            for t in range(4):
+                part = acc[:, t * 128:(t + 1) * 128]
+                if d:
+                    part = part + s_acc[n, t, 0:128]
+                if d == 2:
+                    o[:, n * 512 + t * 128:n * 512 + (t + 1) * 128] = part.astype(bf16)
+                else:
+                    s_acc[n, t, 0:128] = part
+
     acts = {
         "N1": lambda: lax.fori_loop(0, NY, need1, 0), "F": find_slots, "O": put_own, "R": ring, "P": rounds, "C": collect,
         "S": sib_in, "U": lambda a, b: lax.fori_loop(a, b, unit, 0), "W": w_start, "X": w_forward,
         "V": None,
     }
     acts["D"] = drain
+    acts["J"] = project
+    acts["B"] = lambda: pl.semaphore_wait(bar, len(peers))
     acts["V"] = values
     acts["L"] = w_last
-    acts["I"] = w_in
     acts["H"] = w_share
     acts["G"] = w_shared
     for step in STEPS:
         acts[step[0]](*step[1:])
     started = {a[0] for a in STEPS}
     has = {a[:2] for a in STEPS}
-    own_w.wait()
-    for d in range(1, NX if "V" in started else 0):
-        send_att(d).wait_recv()
-
-    def project(n, _):
-        cols = pl.ds(pl.multiple_of(n * 512, 512), 512)
-        acc = jnp.dot(attg[0], wbuf[0, :, cols], preferred_element_type=f32)
-        for i in range(1, NX):
-            acc = acc + jnp.dot(attg[i], wbuf[i, :, cols], preferred_element_type=f32)
-        o[:, cols] = acc.astype(bf16)
-        return 0
-
-    lax.fori_loop(0, 8, project, 0)
-
     for k in range(2):
         if ("R", k) in has:
             for way in range(2):

time: 82.2 us -> 80 us (0.973)
  Pallas kernels: 79.8 us -> 77.5 us
    pallas_call x1, Pallas kernels: 79.8 us -> 77.5 us  [body(): pl.pallas_call(kernel, out_shape=jax.ShapeDtypeStruct((128, 4096), bf16),...]
where the time goes in v3:
time: 80 us; the launch traced here: 79.8 us
  Pallas kernels  77.5 us (97%)
  local copies, waits for them, and re-layouts  2.29 us (3%)
    pallas_call x1, Pallas kernels, body(): pl.pallas_call(kernel, out_shape=jax.ShapeDtypeStruct((128, 4096), bf16),...  77.5 us
    unnamed x1, local copies, waits for them, and re-layouts  2.29 us

profile of v3, /device:TPU:1, one launch (start us, length us, event | category | flops | bytes accessed | tf_op | source)
XLA Modules:
  0.0 79.8 jit_solution(14470807346877588427)
XLA Ops:
  0.0 77.5 %block_attention.1 = bf16[128,4096]{1,0:T(8,128)(2,1)} custom-call(s32[8,64]{1,0:T(8,128)} %bitcast.3, s32[32]{0:T(128)} %pb.1, bf16[512,512]{1,0:T(8,128)(2,1)} %q.1, bf16[2,2,256,128]{3,2,1,0:T(8,128)(2,1)} %bitcast.2, bf16[512,4096]{1,0:T(8,128)(2,1)} %w.1), custom_call_target="tpu_custom_call" | custom-call | flops 6442450944 | bytes 8388608 | tf_op jit(solution)/shard_map/block_attention/pallas_call | solution.py:363
  77.5 2.3 %copy.7 = bf16[128,4096]{1,0:T(8,128)(2,1)} copy(bf16[128,4096]{1,0:T(8,128)(2,1)} %block_attention.1) | data formatting | bytes 2097152
